TPU v7x, 32 devices: a whole 2x2x4 slice. The times are simulated.
32 devices in a mesh: groups: 2 (over y), loop: 16 (over z, x, core).
Axes of the slice: x: 2, y: 2, z: 4, core: 2. Of those that a mesh axis runs over, the one named last changes fastest.
Arguments:
- store: bfloat16 [384, 9216], P(('groups', 'loop')), parts along dimension 0
- source: int32 [384], P(('groups', 'loop')), parts along dimension 0, may hold values from 0 to 191, each once
- lengths: int32 [12], P('groups'), parts along dimension 0, may hold values from 1 to 96, 192 in all
- block_table: int32 [72], P('groups'), parts along dimension 0, may hold values from 0 to 35, each once
- ln_gain: float32 [9216], replicated, may hold values from 0.1 to 1.9
- ln_bias: float32 [9216], replicated, may hold values from -3 to 3
- kv_weight: bfloat16 [9216, 16384], P(None, 'loop'), may hold values from -0.0625 to 0.0625
- kv_bias: float32 [16384], P('loop'), may hold values from -3 to 3
- cache: bfloat16 [72, 16, 16384], P('groups', None, 'loop'), parts along dimension 0, may hold values from -6 to 6
Outputs:
- cache_out: bfloat16 [72, 16, 16384], P('groups', None, 'loop'), parts along dimension 0
There are 2 independent parts, one for each index of `groups`. A program takes and returns all parts, laid end to end along the dimension named above; an argument that names none is the same for every part. Nothing has to cross between parts.
Inputs may be any that keep to these rules, and one draw needn't show every extreme that they name: source is a permutation of the store rows.
All inputs are finite; a program needn't handle non-finite values.
Results may differ from a plain program's by a relative error of at most 0.0029.
Values may be sent and summed in bfloat16 or wider, within the bound.
A program may use at most 192 MiB of HBM per device.

v0:
```python
import jax
import jax.numpy as jnp
from jax import lax
from jax.sharding import PartitionSpec as P

PAGE = 16


def layer_norm(rows, ln_gain, ln_bias):
    values = rows.astype(jnp.float32)
    center = values - jnp.mean(values, axis=-1, keepdims=True)
    spread = jnp.mean(center * center, axis=-1, keepdims=True)
    return (center * lax.rsqrt(spread + 1e-05) * ln_gain + ln_bias).astype(jnp.bfloat16)


def cache_rows(lengths, block_table, total):
    ends = jnp.cumsum(lengths)
    token = jnp.arange(total, dtype=jnp.int32)
    passed = (token[:, None] >= ends[None, :]).astype(jnp.int32)
    session = jnp.sum(passed, axis=1)
    position = token - jnp.sum(passed * lengths[None, :], axis=1)
    per_session = block_table.shape[0] // lengths.shape[0]
    entry = session * per_session + position // PAGE
    table_ids = jnp.arange(block_table.shape[0], dtype=jnp.int32)
    page = jnp.sum(jnp.where(table_ids[None, :] == entry[:, None], block_table[None, :], 0), axis=1)
    return page * PAGE + position % PAGE


def local(store, source, lengths, block_table, ln_gain, ln_bias, kv_weight, kv_bias, cache):
    rows_dev = store.shape[0]
    devices = lax.axis_size("loop")
    total = rows_dev * devices
    every_source = lax.all_gather(source, "loop", axis=0, tiled=True)
    product = jnp.dot(
        layer_norm(lax.all_gather(store, "loop", axis=0, tiled=True), ln_gain, ln_bias),
        kv_weight,
        preferred_element_type=jnp.float32,
    )
    by_slot = (product + kv_bias).astype(jnp.bfloat16)
    new_rows = jnp.take(by_slot, every_source, axis=0)
    dest = cache_rows(lengths, block_table, total)
    flat = cache.reshape(cache.shape[0] * cache.shape[1], cache.shape[2])
    return flat.at[dest].set(new_rows).reshape(cache.shape)


def solution(mesh):
    placed = (
        P(("groups", "loop"), None),
        P(("groups", "loop")),
        P("groups"),
        P("groups"),
        P(),
        P(),
        P(None, "loop"),
        P("loop"),
        P("groups", None, "loop"),
    )
    return jax.shard_map(
        local, mesh=mesh, in_specs=placed, out_specs=P("groups", None, "loop"), check_vma=False
    )
```

profile of v0, /device:TPU:0, one launch (start us, length us, event | category | flops | bytes accessed | tf_op | source)
XLA Modules:
  0.0 102.0 jit_solution(1504740793586261721)
XLA Ops:
  6.5 0.0 all-gather.3.cloned.1.call-start
  6.5 0.7 all-gather.3.cloned.1.call-update
  7.3 0.8 reduce-window.8
  8.1 1.2 %dynamic-slice = u32[1]{0:T(128)} dynamic-slice(u32[32]{0:T(128)} %constant.66, u32[]{:T(128)S(6)} %add.96), dynamic_slice_sizes={1} | dynamic-slice | bytes 12
  10.0 0.9 dynamic-update-slice
  10.9 13.8 %all-reduce = s32[192]{0:T(256)S(1)} all-reduce(s32[192]{0:T(256)S(1)} %dynamic-update-slice), channel_id=1, replica_groups=mesh['groups'=2,'loop'=16] {'loop'}, use_global_device_ids=true, to_apply=%add | all-reduce | flops 192 | bytes 1536
  24.7 0.7 convert_reduce_fusion.1
  25.4 0.7 select_reduce_fusion
  26.2 39.5 %all-gather.3.cloned.1.call-done = bf16[16,12,9216]{2,1,0:T(8,128)(2,1)} async-done(((bf16[1,12,9216]{2,1,0:T(8,128)(2,1)}), bf16[16,12,9216]{2,1,0:T(8,128)(2,1)}) %all-gather.3.cloned.1.call-update) | async-done | bytes 3538960 | tf_op jit(solution)/shard_map/all_gather | solution.py:35
  65.8 3.2 %convert_reduce_fusion = f32[16,12]{1,0:T(8,128)S(1)} fusion(bf16[16,12,9216]{2,1,0:T(8,128)(2,1)} %all-gather.3.cloned.1.call-done), kind=kLoop, calls=%fused_computation.9 | loop fusion | flops 3538752 | bytes 3539712 | tf_op jit(solution)/shard_map/reduce_sum | solution.py:11
  69.0 0.1 reshape.171
  69.1 0.0 copy-start.3
  69.1 0.0 copy-start.4
  69.1 0.0 copy-start.5
  69.1 5.9 %reshape.166 = f32[192,9216]{1,0:T(8,128)} reshape(bf16[16,12,9216]{2,1,0:T(8,128)(2,1)} %all-gather.3.cloned.1.call-done) | data formatting | bytes 10616832 | tf_op jit(solution)/shard_map/convert_element_type | solution.py:10
  75.0 0.0 copy-start
  75.0 4.0 %multiply_reduce_fusion = f32[192]{0:T(256)S(1)} fusion(f32[192,9216]{1,0:T(8,128)} %reshape.166, f32[192]{0:T(256)S(1)} %reshape.171), kind=kLoop, calls=%fused_computation.3 | loop fusion | flops 5308224 | bytes 7079424 | tf_op jit(solution)/shard_map/reduce_sum | solution.py:12
  79.0 0.0 copy-done.3
  79.1 0.0 copy-done.4
  79.1 0.0 copy-done.5
  79.1 1.0 copy-done
  80.0 0.0 copy-start.2
  80.0 10.6 %fusion.6 = bf16[192,1024]{1,0:T(8,128)(2,1)S(1)} fusion(bf16[9216,1024]{1,0:T(8,128)(2,1)} %param.15, f32[192,9216]{1,0:T(8,128)S(1)} %copy-done, f32[9216]{0:T(1024)S(1)} %copy-done.3, f32[9216]{0:T(1024)S(1)} %copy-done.4, f32[192]{0:T(256)S(1)} %add_rsqrt_fusion, f32[192]{0:T(256)S(1)} %reshape.171, f32[1024]{0:T(1024)S(1)} %copy-done.5), kind=kOutput, calls=%fused_computation.11 | convolution fusion | flops 3633119232 | bytes 26424832 | tf_op jit(solution)/shard_map/dot_general | solution.py:34
  90.7 0.0 copy-done.2
  90.7 3.5 %scatter_custom_fusion = bf16[576,1024]{1,0:T(8,128)(2,1)S(1)} fusion(bf16[576,1024]{1,0:T(8,128)(2,1)S(1)} %bitcast.10, s32[192]{0:T(256)S(1)} %bitcast.14, pred[192]{0:T(512)(128)(4,1)S(1)} %compare_and_fusion, bf16[]{:T(256)} %constant.61.clone.1, bf16[192,1024]{1,0:T(8,128)(2,1)S(1)} %fusion.6, s32[1024]{0:T(1024)S(1)} %pad_clamp_fusion), kind=kCustom, calls=%fused_computation.12 | custom fusion | flops 196608 | bytes 1577474 | tf_op jit(solution)/shard_map/scatter | solution.py:43
  94.2 0.0 copy-start.1
  94.2 1.0 copy-done.1
  (9 shorter events, 0.1 us)
Async XLA Ops:
  6.5 59.2 %all-gather.3.cloned.1.call-start = ((), (), s32[]{:S(2)}) async-start(), calls=%async_computation | async-start | bytes 5013504 | tf_op jit(solution)/shard_map/all_gather | solution.py:35
  69.1 10.0 %copy-start.3 = (f32[9216]{0:T(1024)S(1)}, f32[9216]{0:T(1024)}, u32[]{:S(2)}) copy-start(f32[9216]{0:T(1024)} %param.14) | copy-start | bytes 110596
  69.1 10.0 %copy-start.4 = (f32[9216]{0:T(1024)S(1)}, f32[9216]{0:T(1024)}, u32[]{:S(2)}) copy-start(f32[9216]{0:T(1024)} %param.13) | copy-start | bytes 110596
  69.1 10.0 %copy-start.5 = (f32[1024]{0:T(1024)S(1)}, f32[1024]{0:T(1024)}, u32[]{:S(2)}) copy-start(f32[1024]{0:T(1024)} %param.16) | copy-start | bytes 12292
  75.0 5.0 %copy-start = (f32[192,9216]{1,0:T(8,128)S(1)}, f32[192,9216]{1,0:T(8,128)}, u32[]{:S(2)}) copy-start(f32[192,9216]{1,0:T(8,128)} %reshape.166) | copy-start | bytes 21233668
  80.0 10.6 %copy-start.2 = (bf16[36,16,1024]{2,1,0:T(8,128)(2,1)S(1)}, bf16[36,16,1024]{2,1,0:T(8,128)(2,1)}, u32[]{:S(2)}) copy-start(bf16[36,16,1024]{2,1,0:T(8,128)(2,1)} %param.17) | copy-start | bytes 3538948
  94.2 1.0 copy-start.1
Sparse Core Ops, SparseCore 0:
  9.6 56.0 all-gather.2
where the time goes:
time: 102 us
  waiting for transfers between devices  40.3 us (40%)
  between operations  14.2 us (14%)
  blocking collectives  13.8 us (14%)
  other arithmetic  13.1 us (13%)
  matrix products  10.6 us (10%)
  local copies, waits for them, and re-layouts  10.1 us (10%)
    all_gather x1, waiting for transfers between devices, local(): lax.all_gather(store, 'loop', axis=0, tiled=True)  39.5 us
    unnamed x1, blocking collectives  13.8 us
    dot_general x1, matrix products, local(): jnp.dot(layer_norm(lax.all_gather(store, 'loop', axis=0, tiled=True), ln_...  10.6 us
    convert_element_type x1, local copies, waits for them, and re-layouts, layer_norm(): values = rows.astype(jnp.float32)  5.91 us
    unnamed x14, local copies, waits for them, and re-layouts  4.09 us
    reduce_sum x1, other arithmetic, layer_norm(): spread = jnp.mean(center * center, axis=-1, keepdims=True)  4.02 us
    scatter x1, other arithmetic, local(): return flat.at[dest].set(new_rows).reshape(cache.shape)  3.48 us
    reduce_sum x1, other arithmetic, layer_norm(): center = values - jnp.mean(values, axis=-1, keepdims=True)  3.19 us
  transfers between devices with their start and end apart: 1, of which 1 were waited for; matrix products, arithmetic and copies ran while one was open for 4% of the time, Pallas kernels for 0%

commit v1 on v0

--- a/solution.py
+++ b/solution.py
@@ -1,6 +1,8 @@
 import jax
 import jax.numpy as jnp
 from jax import lax
+from jax.experimental import pallas as pl
+from jax.experimental.pallas import tpu as pltpu
 from jax.sharding import PartitionSpec as P
 
 PAGE = 16
@@ -26,13 +28,337 @@
     return page * PAGE + position % PAGE
 
 
+SEGS = 6
+RING = 8
+MESH = pl.DeviceIdType.MESH
+
+
+def kernel(
+    store, source, lengths, table, gain, bias, weight, kv_bias, cache, out,
+    normed, packed, rows, held, extra, total, every, spread, pages, meta,
+    to_right, to_left, to_twin, from_ring, from_twin,
+    meta_right, meta_left, meta_twin, meta_ring, meta_from_twin,
+    weight_sem, cache_sem, out_sem,
+):
+    count, width = store.shape
+    main = width * 3 // 4
+    seg_width, third = main // SEGS, width // 4
+    half = SEGS // 2
+    features = kv_bias.shape[1]
+    slots = 2 * RING * 16
+    pages_rows = pages.shape[0]
+
+    me = lax.axis_index("loop")
+    core, chip = lax.rem(me, 2), me // 2
+    side = RING // 2
+    place = chip // 2 + lax.rem(chip, 2) * (RING - 1 - 2 * (chip // 2))
+
+    def device(step, which):
+        at = lax.rem(place + step + RING, RING)
+        column = at // side
+        line = at + column * (RING - 1 - 2 * at)
+        return 2 * (2 * line + column) + which
+
+    right, left, twin = device(1, core), device(-1, core), device(0, 1 - core)
+
+    parts = weight_sem.shape[0]
+    depth = width // parts
+
+    def weight_copy(i):
+        span = pl.ds(pl.multiple_of(i * depth, depth), depth)
+        return pltpu.make_async_copy(weight.at[span], held.at[span], weight_sem.at[i])
+
+    barrier = pltpu.get_barrier_semaphore()
+    for other in (right, left, twin):
+        pl.semaphore_signal(barrier, inc=1, device_id={"loop": other}, device_id_type=MESH)
+    for i in range(parts):
+        weight_copy(i).start()
+    cache_copy = pltpu.make_async_copy(cache, pages, cache_sem)
+    cache_copy.start()
+
+    values = store[...].astype(jnp.float32)
+    center = values - jnp.mean(values, axis=-1, keepdims=True)
+    var = jnp.mean(center * center, axis=-1, keepdims=True)
+    normed[0:count, :] = center * lax.rsqrt(var + 1e-05) * gain[...] + bias[...]
+    packed[0:count, :] = normed[0:count, 0:main]
+    for s in range(3):
+        packed[12:16, s * third:(s + 1) * third] = normed[4 * s:4 * s + 4, main:width]
+
+    def row(m, which):
+        return pl.multiple_of((2 * m + which) * 16, 16)
+
+    rows[pl.ds(row(0, core), 16), :] = packed[...].astype(jnp.bfloat16)
+
+    line = lax.broadcasted_iota(jnp.int32, (16, 128), 0)
+    marks = jnp.full((16, 128), -1, jnp.int32)
+    for i in range(count):
+        marks = jnp.where(line == i, source[i], marks)
+
+    def meta_at(dev):
+        return meta.at[pl.ds(pl.multiple_of(dev * 16, 16), 16)]
+
+    meta[pl.ds(pl.multiple_of(me * 16, 16), 16), :] = marks.astype(jnp.float32).astype(jnp.bfloat16)
+
+    def block(m, seg):
+        return rows.at[pl.ds(row(m, core), 16), pl.ds(pl.multiple_of(seg * seg_width, 128), seg_width)]
+
+    def remote(src, dst, send, recv, dev):
+        return pltpu.make_async_remote_copy(
+            src_ref=src, dst_ref=dst, send_sem=send, recv_sem=recv,
+            device_id={"loop": dev}, device_id_type=MESH,
+        )
+
+    def right_copy(k, seg):
+        return remote(
+            block(2 * k - 1 if k else 0, seg), block(2 * k + 1, seg),
+            to_right.at[k, seg], from_ring.at[0, k, seg], right,
+        )
+
+    def left_copy(k, seg):
+        return remote(
+            block(2 * k, seg), block(2 * k + 2 if k < 3 else 7, seg),
+            to_left.at[k, seg], from_ring.at[1, k, seg], left,
+        )
+
+    def twin_copy(m, seg):
+        return remote(block(m, seg), block(m, seg), to_twin.at[m, seg], from_twin.at[m, seg], twin)
+
+    def meta_copy(way, k, owner):
+        sends = (meta_right, meta_left)[way]
+        ref = meta_at(device(owner, core))
+        return remote(ref, ref, sends.at[k], meta_ring.at[way, k], (right, left)[way])
+
+    def meta_twin_copy(m, owner, which):
+        ref = meta_at(device(owner, which))
+        return remote(ref, ref, meta_twin.at[m], meta_from_twin.at[m], twin)
+
+    pl.semaphore_wait(barrier, 3)
+
+    @pl.loop(0, SEGS)
+    def _(seg):
+        right_copy(0, seg).start()
+        left_copy(0, seg).start()
+        twin_copy(0, seg).start()
+
+    meta_copy(0, 0, 0).start()
+    meta_copy(1, 0, 0).start()
+    meta_twin_copy(0, 0, core).start()
+
+    total[...] = jnp.zeros_like(total)
+    extra[...] = jnp.zeros_like(extra)
+
+    def multiply(base, size, seg):
+        cols = pl.ds(pl.multiple_of(seg * seg_width, 128), seg_width)
+        deep = pl.ds(pl.multiple_of(seg * seg_width, seg_width), seg_width)
+        total[base:base + size, :] += jnp.dot(
+            rows[base:base + size, cols], held[deep, :], preferred_element_type=jnp.float32
+        )
+
+    def finish(base, size, owners):
+        for b in range(size // 16):
+            for s in range(3):
+                piece = rows[base + 16 * b:base + 16 * b + 16, s * third:(s + 1) * third]
+                extra[16 * b + 4 * s:16 * b + 4 * s + 4, :] = piece.astype(jnp.float32)[12:16]
+        result = total[base:base + size, :] + jnp.dot(
+            extra[0:size, :].astype(jnp.bfloat16), held[main:width, :],
+            preferred_element_type=jnp.float32,
+        )
+        result = (result + kv_bias[...]).astype(jnp.bfloat16)
+        for b in range(size // 16):
+            dev = device(owners[b // 2], b % 2)
+            every[pl.ds(pl.multiple_of(dev * 16, 16), 16), :] = result[16 * b:16 * b + 16]
+
+    def group(k):
+        if k == 0:
+            return (0,), 0, 32, (0,)
+        if k == 4:
+            return (7,), 224, 32, (-4,)
+        return (2 * k - 1, 2 * k), (2 * k - 1) * 32, 64, (-k, k)
+
+    def work(k, seg):
+        members, base, size, _ = group(k)
+        for m in members:
+            twin_copy(m, seg).wait_recv()
+        if k == 0:
+            weight_copy(seg).wait()
+        multiply(base, size, seg)
+
+    for k in range(1, 4):
+        @pl.loop(0, SEGS)
+        def _(seg, k=k):
+            right_copy(k - 1, seg).wait_recv()
+            if k < 3:
+                right_copy(k, seg).start()
+            else:
+                @pl.when(seg < half)
+                def _():
+                    right_copy(k, seg).start()
+            twin_copy(2 * k - 1, seg).start()
+            left_copy(k - 1, seg).wait_recv()
+            if k < 3:
+                left_copy(k, seg).start()
+            else:
+                @pl.when(seg >= half)
+                def _():
+                    left_copy(k, seg).start()
+            twin_copy(2 * k, seg).start()
+            work(k - 1, seg)
+
+        meta_copy(0, k - 1, -k).wait_recv()
+        meta_copy(0, k, -k).start()
+        meta_twin_copy(2 * k - 1, -k, core).start()
+        meta_copy(1, k - 1, k).wait_recv()
+        if k < 3:
+            meta_copy(1, k, k).start()
+        meta_twin_copy(2 * k, k, core).start()
+        if k == 1:
+            for i in range(SEGS, parts):
+                weight_copy(i).wait()
+        _, base, size, owners = group(k - 1)
+        finish(base, size, owners)
+
+    meta_copy(0, 3, -4).wait_recv()
+    meta_twin_copy(7, -4, core).start()
+
+    @pl.loop(0, half)
+    def _(j):
+        right_copy(3, j).wait_recv()
+        twin_copy(7, j).start()
+        left_copy(3, j + half).wait_recv()
+        twin_copy(7, j + half).start()
+        work(3, 2 * j)
+        work(3, 2 * j + 1)
+
+    _, base, size, owners = group(3)
+    finish(base, size, owners)
+
+    for m, owner in ((0, 0), (1, -1), (2, 1), (3, -2), (4, 2), (5, -3), (6, 3), (7, -4)):
+        meta_twin_copy(m, owner, 1 - core).wait_recv()
+    slot = lax.broadcasted_iota(jnp.int32, (1, slots), 1)
+    index = (slot // 16) * count + lax.rem(slot, 16)
+    real = lax.rem(slot, 16) < count
+    wanted = jnp.where(real, index, -2).astype(jnp.float32)
+    asked = meta[...].astype(jnp.float32)
+    asked = jnp.concatenate([asked] * (slots // 128), axis=1)
+    pick = jnp.where(asked == wanted, 1.0, 0.0).astype(jnp.bfloat16)
+    sessions, entries = lengths.shape[0], table.shape[0]
+    session = jnp.zeros_like(index)
+    position = index
+    end = jnp.int32(0)
+    for s in range(sessions):
+        end = end + lengths[s]
+        passed = index >= end
+        session = session + jnp.where(passed, 1, 0)
+        position = position - jnp.where(passed, lengths[s], 0)
+    entry = session * (entries // sessions) + lax.shift_right_logical(position, 4)
+    page = jnp.zeros_like(index)
+    for e in range(entries):
+        page = jnp.where(entry == e, table[e], page)
+    dest = jnp.where(real, page * PAGE + jnp.bitwise_and(position, PAGE - 1), -1)
+    where = lax.broadcasted_iota(jnp.int32, (pages_rows, slots), 0)
+    put = jnp.where(where == dest, 1.0, 0.0).astype(jnp.bfloat16)
+    spread[...] = jnp.dot(put, pick, preferred_element_type=jnp.float32).astype(jnp.bfloat16)
+    cache_copy.wait()
+
+    @pl.loop(0, half)
+    def _(j):
+        work(4, j)
+        work(4, j + half)
+
+    _, base, size, owners = group(4)
+    finish(base, size, owners)
+
+    chunks = out_sem.shape[0]
+    high = pages_rows // chunks
+
+    def out_copy(i):
+        span = pl.ds(pl.multiple_of(i * high, 16), high)
+        return pltpu.make_async_copy(pages.at[span], out.at[span], out_sem.at[i])
+
+    @pl.loop(0, chunks)
+    def _(i):
+        span = pl.ds(pl.multiple_of(i * high, 16), high)
+        choice = spread[span, :]
+        new = jnp.dot(choice, every[...], preferred_element_type=jnp.float32)
+        taken = jnp.sum(choice.astype(jnp.float32), axis=1, keepdims=True) > 0.5
+        pages[span, :] = jnp.where(taken, new, pages[span, :].astype(jnp.float32)).astype(jnp.bfloat16)
+        out_copy(i).start()
+
+    for k in range(4):
+        @pl.loop(0, half if k == 3 else SEGS)
+        def _(seg, k=k):
+            right_copy(k, seg).wait_send()
+            left_copy(k, seg + half if k == 3 else seg).wait_send()
+        meta_copy(0, k, -k).wait_send()
+        if k < 3:
+            meta_copy(1, k, k).wait_send()
+    for m, owner in ((0, 0), (1, -1), (2, 1), (3, -2), (4, 2), (5, -3), (6, 3), (7, -4)):
+        meta_twin_copy(m, owner, core).wait_send()
+
+        @pl.loop(0, SEGS)
+        def _(seg, m=m):
+            twin_copy(m, seg).wait_send()
+
+    @pl.loop(0, chunks)
+    def _(i):
+        out_copy(i).wait()
+
+
+def fused(store, source, lengths, table, ln_gain, ln_bias, kv_weight, kv_bias, cache):
+    count, width = store.shape
+    features = kv_weight.shape[1]
+    pages_rows = cache.shape[0] * cache.shape[1]
+    slots = 2 * RING * 16
+    parts, chunks = 8, 6
+    vmem, smem, hbm = (
+        pl.BlockSpec(memory_space=pltpu.VMEM),
+        pl.BlockSpec(memory_space=pltpu.SMEM),
+        pl.BlockSpec(memory_space=pltpu.HBM),
+    )
+    dma = pltpu.SemaphoreType.DMA
+    result = pl.pallas_call(
+        kernel,
+        out_shape=jax.ShapeDtypeStruct((pages_rows, features), jnp.bfloat16),
+        in_specs=[vmem, smem, smem, smem, vmem, vmem, hbm, vmem, hbm],
+        out_specs=hbm,
+        scratch_shapes=[
+            pltpu.VMEM((16, width), jnp.float32),
+            pltpu.VMEM((16, width * 3 // 4), jnp.float32),
+            pltpu.VMEM((slots, width * 3 // 4), jnp.bfloat16),
+            pltpu.VMEM((width, features), jnp.bfloat16),
+            pltpu.VMEM((64, width // 4), jnp.float32),
+            pltpu.VMEM((slots, features), jnp.float32),
+            pltpu.VMEM((slots, features), jnp.bfloat16),
+            pltpu.VMEM((pages_rows, slots), jnp.bfloat16),
+            pltpu.VMEM((pages_rows, features), jnp.bfloat16),
+            pltpu.VMEM((slots, 128), jnp.bfloat16),
+            dma((4, SEGS)), dma((4, SEGS)), dma((8, SEGS)), dma((2, 4, SEGS)), dma((8, SEGS)),
+            dma((4,)), dma((4,)), dma((8,)), dma((2, 4)), dma((8,)),
+            dma((parts,)), dma, dma((chunks,)),
+        ],
+        compiler_params=pltpu.CompilerParams(
+            collective_id=0, has_side_effects=True, vmem_limit_bytes=56 * 1024 * 1024
+        ),
+        cost_estimate=pl.CostEstimate(
+            flops=2 * slots * width * features, transcendentals=0,
+            bytes_accessed=2 * width * features + 4 * pages_rows * features,
+        ),
+    )(
+        store, source, lengths, table, ln_gain.reshape(1, width), ln_bias.reshape(1, width),
+        kv_weight, kv_bias.reshape(1, features), cache.reshape(pages_rows, features),
+    )
+    return result.reshape(cache.shape)
+
+
 def local(store, source, lengths, block_table, ln_gain, ln_bias, kv_weight, kv_bias, cache):
     rows_dev = store.shape[0]
     devices = lax.axis_size("loop")
     total = rows_dev * devices
+    if devices == 2 * RING and rows_dev == 12:
+        return fused(store, source, lengths, block_table, ln_gain, ln_bias, kv_weight, kv_bias, cache)
     every_source = lax.all_gather(source, "loop", axis=0, tiled=True)
     product = jnp.dot(
-        layer_norm(lax.all_gather(store, "loop", axis=0, tiled=True), ln_gain, ln_bias),
+        lax.all_gather(layer_norm(store, ln_gain, ln_bias), "loop", axis=0, tiled=True),
         kv_weight,
         preferred_element_type=jnp.float32,
     )

time: 102 us -> 39.9 us (0.39)
  waiting for transfers between devices: 40.3 us -> 0 us
  Pallas kernels: 0 us -> 37.3 us
  between operations: 14.2 us -> 0.01 us
  blocking collectives: 13.8 us -> 0 us
  other arithmetic: 13.1 us -> 0 us
  matrix products: 10.6 us -> 0 us
  local copies, waits for them, and re-layouts: 10.1 us -> 2.42 us
    all_gather x1 -> x0, waiting for transfers between devices: 39.5 us -> none  [local(): lax.all_gather(store, 'loop', axis=0, tiled=True)]
    pallas_call x0 -> x1, Pallas kernels: none -> 37.3 us  [fused(): pl.pallas_call(kernel, out_shape=jax.ShapeDtypeStruct((pages_rows, featur...]
    unnamed x1 -> x0, blocking collectives: 13.8 us -> none
    dot_general x1 -> x0, matrix products: 10.6 us -> none  [local(): jnp.dot(layer_norm(lax.all_gather(store, 'loop', axis=0, tiled=True), ln_...]
    reduce_sum x4 -> x0, other arithmetic: 8.7 us -> none  [the longest x1 4.02 us: layer_norm(): spread = jnp.mean(center * center, axis=-1, keepdims=True)]
    convert_element_type x1 -> x0, local copies, waits for them, and re-layouts: 5.91 us -> none  [layer_norm(): values = rows.astype(jnp.float32)]
    scatter x1 -> x0, other arithmetic: 3.48 us -> none  [local(): return flat.at[dest].set(new_rows).reshape(cache.shape)]
    unnamed x14 -> x1, local copies, waits for them, and re-layouts: 4.09 us -> 2.42 us
  transfers between devices with their start and end apart: 1 -> 0, of which waited for: 1 -> 0; matrix products, arithmetic and copies ran while one was open for 4% -> 0% of each run, Pallas kernels for 0% -> 0%
where the time goes in v1:
time: 39.9 us; the launch traced here: 39.7 us
  Pallas kernels  37.3 us (93%)
  local copies, waits for them, and re-layouts  2.42 us (6%)
    pallas_call x1, Pallas kernels, fused(): pl.pallas_call(kernel, out_shape=jax.ShapeDtypeStruct((pages_rows, featur...  37.3 us
    unnamed x1, local copies, waits for them, and re-layouts  2.42 us

profile of v1, /device:TPU:0, one launch (start us, length us, event | category | flops | bytes accessed | tf_op | source)
XLA Modules:
  0.0 39.7 jit_solution(11081773544529323935)
XLA Ops:
  0.0 37.3 %shard_map.91 = bf16[576,1024]{1,0:T(8,128)(2,1)} custom-call(bf16[12,9216]{1,0:T(8,128)(2,1)} %store.1, s32[12]{0:T(128)} %source.1, s32[6]{0:T(128)} %lengths.1, s32[36]{0:T(128)} %table.1, f32[1,9216]{1,0:T(1,128)} %bitcast.7, f32[1,9216]{1,0:T(1,128)} %bitcast.8, bf16[9216,1024]{1,0:T(8,128)(2,1)} %weight.1, f32[1,1024]{1,0:T(1,128)} %bitcast.9, ...), custom_call_target="tpu_custom_call" | custom-call | flops 4831838208 | bytes 21233664 | tf_op jit(solution)/shard_map/pallas_call | solution.py:319
  37.3 2.4 %copy.11 = bf16[36,16,1024]{2,1,0:T(8,128)(2,1)} copy(bf16[36,16,1024]{2,1,0:T(8,128)(2,1)} %bitcast.5) | data formatting | bytes 2359296

commit v2 on v1

--- a/solution.py
+++ b/solution.py
@@ -134,18 +134,28 @@
 
     pl.semaphore_wait(barrier, 3)
 
-    @pl.loop(0, SEGS)
-    def _(seg):
-        right_copy(0, seg).start()
-        left_copy(0, seg).start()
-        twin_copy(0, seg).start()
+    @pl.loop(0, half)
+    def _(j):
+        right_copy(0, j).start()
+        left_copy(0, j + half).start()
 
     meta_copy(0, 0, 0).start()
     meta_copy(1, 0, 0).start()
     meta_twin_copy(0, 0, core).start()
 
+    @pl.loop(0, SEGS)
+    def _(seg):
+        twin_copy(0, seg).start()
+
     total[...] = jnp.zeros_like(total)
     extra[...] = jnp.zeros_like(extra)
+
+    @pl.loop(0, half)
+    def _(j):
+        right_copy(0, j).wait_send()
+        right_copy(0, j + half).start()
+        left_copy(0, j + half).wait_send()
+        left_copy(0, j).start()
 
     def multiply(base, size, seg):
         cols = pl.ds(pl.multiple_of(seg * seg_width, 128), seg_width)
@@ -154,11 +164,14 @@
             rows[base:base + size, cols], held[deep, :], preferred_element_type=jnp.float32
         )
 
-    def finish(base, size, owners):
+    def collect(base, size, at):
         for b in range(size // 16):
             for s in range(3):
                 piece = rows[base + 16 * b:base + 16 * b + 16, s * third:(s + 1) * third]
-                extra[16 * b + 4 * s:16 * b + 4 * s + 4, :] = piece.astype(jnp.float32)[12:16]
+                spot = at + 16 * b + 4 * s
+                extra[spot:spot + 4, :] = piece.astype(jnp.float32)[12:16]
+
+    def finish(base, size, owners):
         result = total[base:base + size, :] + jnp.dot(
             extra[0:size, :].astype(jnp.bfloat16), held[main:width, :],
             preferred_element_type=jnp.float32,
@@ -168,42 +181,11 @@
             dev = device(owners[b // 2], b % 2)
             every[pl.ds(pl.multiple_of(dev * 16, 16), 16), :] = result[16 * b:16 * b + 16]
 
-    def group(k):
-        if k == 0:
-            return (0,), 0, 32, (0,)
-        if k == 4:
-            return (7,), 224, 32, (-4,)
-        return (2 * k - 1, 2 * k), (2 * k - 1) * 32, 64, (-k, k)
-
-    def work(k, seg):
-        members, base, size, _ = group(k)
+    def arrived(members, seg):
         for m in members:
             twin_copy(m, seg).wait_recv()
-        if k == 0:
-            weight_copy(seg).wait()
-        multiply(base, size, seg)
 
     for k in range(1, 4):
-        @pl.loop(0, SEGS)
-        def _(seg, k=k):
-            right_copy(k - 1, seg).wait_recv()
-            if k < 3:
-                right_copy(k, seg).start()
-            else:
-                @pl.when(seg < half)
-                def _():
-                    right_copy(k, seg).start()
-            twin_copy(2 * k - 1, seg).start()
-            left_copy(k - 1, seg).wait_recv()
-            if k < 3:
-                left_copy(k, seg).start()
-            else:
-                @pl.when(seg >= half)
-                def _():
-                    left_copy(k, seg).start()
-            twin_copy(2 * k, seg).start()
-            work(k - 1, seg)
-
         meta_copy(0, k - 1, -k).wait_recv()
         meta_copy(0, k, -k).start()
         meta_twin_copy(2 * k - 1, -k, core).start()
@@ -211,26 +193,27 @@
         if k < 3:
             meta_copy(1, k, k).start()
         meta_twin_copy(2 * k, k, core).start()
-        if k == 1:
-            for i in range(SEGS, parts):
-                weight_copy(i).wait()
-        _, base, size, owners = group(k - 1)
-        finish(base, size, owners)
+        for h in range(2):
+            @pl.loop(0, half)
+            def _(j, k=k, h=h):
+                first, second = (j, j + half) if h == 0 else (j + half, j)
+                right_copy(k - 1, first).wait_recv()
+                if k < 3 or h == 0:
+                    right_copy(k - 1 + h, second).wait_send()
+                    right_copy(k, first).start()
+                twin_copy(2 * k - 1, first).start()
+                left_copy(k - 1, second).wait_recv()
+                if k < 3 or h == 0:
+                    left_copy(k - 1 + h, first).wait_send()
+                    left_copy(k, second).start()
+                twin_copy(2 * k, second).start()
+                if k == 3:
+                    arrived(range(5), first)
+                    weight_copy(first).wait()
+                    multiply(0, 160, first)
 
     meta_copy(0, 3, -4).wait_recv()
     meta_twin_copy(7, -4, core).start()
-
-    @pl.loop(0, half)
-    def _(j):
-        right_copy(3, j).wait_recv()
-        twin_copy(7, j).start()
-        left_copy(3, j + half).wait_recv()
-        twin_copy(7, j + half).start()
-        work(3, 2 * j)
-        work(3, 2 * j + 1)
-
-    _, base, size, owners = group(3)
-    finish(base, size, owners)
 
     for m, owner in ((0, 0), (1, -1), (2, 1), (3, -2), (4, 2), (5, -3), (6, 3), (7, -4)):
         meta_twin_copy(m, owner, 1 - core).wait_recv()
@@ -259,14 +242,27 @@
     put = jnp.where(where == dest, 1.0, 0.0).astype(jnp.bfloat16)
     spread[...] = jnp.dot(put, pick, preferred_element_type=jnp.float32).astype(jnp.bfloat16)
     cache_copy.wait()
-
-    @pl.loop(0, half)
-    def _(j):
-        work(4, j)
-        work(4, j + half)
-
-    _, base, size, owners = group(4)
-    finish(base, size, owners)
+    for i in range(SEGS, parts):
+        weight_copy(i).wait()
+    collect(0, 160, 0)
+    finish(0, 160, (0, -1, 1, -2, 2))
+
+    def pair(j):
+        arrived((5, 6, 7), j)
+        arrived((5, 6, 7), j + half)
+        multiply(160, 96, j)
+        multiply(160, 96, j + half)
+
+    for j in range(half):
+        right_copy(3, j).wait_recv()
+        twin_copy(7, j).start()
+        left_copy(3, j + half).wait_recv()
+        twin_copy(7, j + half).start()
+        if j > 0:
+            pair(j - 1)
+    pair(half - 1)
+    collect(160, 96, 0)
+    finish(160, 96, (-3, 3, -4))
 
     chunks = out_sem.shape[0]
     high = pages_rows // chunks
@@ -285,13 +281,15 @@
         out_copy(i).start()
 
     for k in range(4):
-        @pl.loop(0, half if k == 3 else SEGS)
-        def _(seg, k=k):
-            right_copy(k, seg).wait_send()
-            left_copy(k, seg + half if k == 3 else seg).wait_send()
         meta_copy(0, k, -k).wait_send()
         if k < 3:
             meta_copy(1, k, k).wait_send()
+
+    @pl.loop(0, half)
+    def _(j):
+        right_copy(3, j).wait_send()
+        left_copy(3, j + half).wait_send()
+
     for m, owner in ((0, 0), (1, -1), (2, 1), (3, -2), (4, 2), (5, -3), (6, 3), (7, -4)):
         meta_twin_copy(m, owner, core).wait_send()
 
@@ -326,7 +324,7 @@
             pltpu.VMEM((16, width * 3 // 4), jnp.float32),
             pltpu.VMEM((slots, width * 3 // 4), jnp.bfloat16),
             pltpu.VMEM((width, features), jnp.bfloat16),
-            pltpu.VMEM((64, width // 4), jnp.float32),
+            pltpu.VMEM((160, width // 4), jnp.float32),
             pltpu.VMEM((slots, features), jnp.float32),
             pltpu.VMEM((slots, features), jnp.bfloat16),
             pltpu.VMEM((pages_rows, slots), jnp.bfloat16),

time: 39.9 us -> 35.9 us (0.90)
  Pallas kernels: 37.3 us -> 33.3 us
    pallas_call x1, Pallas kernels: 37.3 us -> 33.3 us  [fused(): pl.pallas_call(kernel, out_shape=jax.ShapeDtypeStruct((pages_rows, featur...]
where the time goes in v2:
time: 35.9 us; the launch traced here: 35.7 us
  Pallas kernels  33.3 us (93%)
  local copies, waits for them, and re-layouts  2.42 us (7%)
    pallas_call x1, Pallas kernels, fused(): pl.pallas_call(kernel, out_shape=jax.ShapeDtypeStruct((pages_rows, featur...  33.3 us
    unnamed x1, local copies, waits for them, and re-layouts  2.42 us

profile of v2, /device:TPU:0, one launch (start us, length us, event | category | flops | bytes accessed | tf_op | source)
XLA Modules:
  0.0 35.7 jit_solution(8873735483880491410)
XLA Ops:
  0.0 33.3 %shard_map.91 = bf16[576,1024]{1,0:T(8,128)(2,1)} custom-call(bf16[12,9216]{1,0:T(8,128)(2,1)} %store.1, s32[12]{0:T(128)} %source.1, s32[6]{0:T(128)} %lengths.1, s32[36]{0:T(128)} %table.1, f32[1,9216]{1,0:T(1,128)} %bitcast.7, f32[1,9216]{1,0:T(1,128)} %bitcast.8, bf16[9216,1024]{1,0:T(8,128)(2,1)} %weight.1, f32[1,1024]{1,0:T(1,128)} %bitcast.9, ...), custom_call_target="tpu_custom_call" | custom-call | flops 4831838208 | bytes 21233664 | tf_op jit(solution)/shard_map/pallas_call | solution.py:317
  33.3 2.4 %copy.11 = bf16[36,16,1024]{2,1,0:T(8,128)(2,1)} copy(bf16[36,16,1024]{2,1,0:T(8,128)(2,1)} %bitcast.5) | data formatting | bytes 2359296

commit v3 on v2

--- a/solution.py
+++ b/solution.py
@@ -260,8 +260,14 @@
         twin_copy(7, j + half).start()
         if j > 0:
             pair(j - 1)
-    pair(half - 1)
-    collect(160, 96, 0)
+    arrived((5, 6), half - 1)
+    arrived((5, 6), SEGS - 1)
+    collect(160, 64, 0)
+    arrived((7,), half - 1)
+    arrived((7,), SEGS - 1)
+    collect(224, 32, 64)
+    multiply(160, 96, half - 1)
+    multiply(160, 96, SEGS - 1)
     finish(160, 96, (-3, 3, -4))
 
     chunks = out_sem.shape[0]
@@ -307,7 +313,7 @@
     features = kv_weight.shape[1]
     pages_rows = cache.shape[0] * cache.shape[1]
     slots = 2 * RING * 16
-    parts, chunks = 8, 6
+    parts, chunks = 8, 3
     vmem, smem, hbm = (
         pl.BlockSpec(memory_space=pltpu.VMEM),
         pl.BlockSpec(memory_space=pltpu.SMEM),

time: 35.9 us -> 35.4 us (0.986)
  Pallas kernels: 33.3 us -> 32.8 us
    pallas_call x1, Pallas kernels: 33.3 us -> 32.8 us  [fused(): pl.pallas_call(kernel, out_shape=jax.ShapeDtypeStruct((pages_rows, featur...]
where the time goes in v3:
time: 35.4 us; the launch traced here: 35.3 us
  Pallas kernels  32.8 us (93%)
  local copies, waits for them, and re-layouts  2.42 us (7%)
    pallas_call x1, Pallas kernels, fused(): pl.pallas_call(kernel, out_shape=jax.ShapeDtypeStruct((pages_rows, featur...  32.8 us
    unnamed x1, local copies, waits for them, and re-layouts  2.42 us

profile of v3, /device:TPU:0, one launch (start us, length us, event | category | flops | bytes accessed | tf_op | source)
XLA Modules:
  0.0 35.3 jit_solution(10009115526023154280)
XLA Ops:
  0.0 32.8 %shard_map.91 = bf16[576,1024]{1,0:T(8,128)(2,1)} custom-call(bf16[12,9216]{1,0:T(8,128)(2,1)} %store.1, s32[12]{0:T(128)} %source.1, s32[6]{0:T(128)} %lengths.1, s32[36]{0:T(128)} %table.1, f32[1,9216]{1,0:T(1,128)} %bitcast.7, f32[1,9216]{1,0:T(1,128)} %bitcast.8, bf16[9216,1024]{1,0:T(8,128)(2,1)} %weight.1, f32[1,1024]{1,0:T(1,128)} %bitcast.9, ...), custom_call_target="tpu_custom_call" | custom-call | flops 4831838208 | bytes 21233664 | tf_op jit(solution)/shard_map/pallas_call | solution.py:323
  32.8 2.4 %copy.11 = bf16[36,16,1024]{2,1,0:T(8,128)(2,1)} copy(bf16[36,16,1024]{2,1,0:T(8,128)(2,1)} %bitcast.5) | data formatting | bytes 2359296
